TPU v7x, 256 devices: a whole 4x4x8 slice. The times are simulated.
256 devices in a mesh: panel: 2 (over x_hi), lat: 4 (over y), lon: 32 (over z, x_lo, core).
Axes of the slice: x: 4 (x_hi: 2, x_lo: 2; x = x_hi * 2 + x_lo), y: 4, z: 8, core: 2. Of those that a mesh axis runs over, the one named last changes fastest.
Arguments:
- fields: float32 [2, 8, 256, 49152], P('panel', None, 'lat', 'lon'), may hold values from -6 to 6
- coupling: float32 [4, 8, 8], replicated, may hold values from -4 to 4
- export_index: int32 [2, 4, 32, 512], P('panel', 'lat', 'lon'), may hold values from 0 to 767, as said below
- ghost_ns_index: int32 [2, 2, 2, 384, 4], P('panel', None, None, 'lon'), may hold values from 0 to 511
- ghost_ns_frac: float32 [2, 2, 2, 384, 2], P('panel', None, None, 'lon'), may hold values from 0.32 to 0.68
- ghost_ew_index: int32 [2, 2, 256, 2, 4], P('panel', None, 'lat'), may hold values from 0 to 511
- ghost_ew_frac: float32 [2, 2, 256, 2, 2], P('panel', None, 'lat'), may hold values from 0.32 to 0.68
Outputs:
- advanced: float32 [2, 8, 256, 49152], P('panel', None, 'lat', 'lon')
Inputs may be any that keep to these rules, and one draw needn't show every extreme that they name: `export_index`: local column of the sending device's block. `ghost_ns_index`: received slot: source position times 4 plus the slot number. `ghost_ew_index`: received slot: source position times 4 plus the slot number.
All inputs are finite; a program needn't handle non-finite values.
Results may differ from a plain program's by a relative error of at most 0.0001.
Values sent between devices are 32-bit elements; how exact they have to be, the bound alone decides.
A program may use at most 64 MiB of HBM per device.

v0:
```python
import functools
import math

import jax
import jax.numpy as jnp
from jax import lax
from jax.experimental import pallas as pl
from jax.experimental.pallas import tpu as pltpu
from jax.sharding import PartitionSpec as P

NR = 128
FIELDS = 8
LAT_DEV = 64
LON_DEV = 12
N_LAT = 4
N_LON = 32
N_Z = 8

time_step = 0.15
viscosity = 0.1
inner_radius = 0.35

MESH = pl.DeviceIdType.MESH
TILE = (FIELDS, NR)


def kernel(
    x_ref, coup_ref, nsi_ref, nsw_ref, exp_ref, ewi_ref, eww_ref, isin_ref,
    out_ref,
    q_init, q_mid, p_lat, p_lon, s_ref, res_ref, lhs_ref,
    send_g, recv_g0, recv_g1, send_e, recv_e1, recv_e20, recv_e21, chunk, recv_n, lat_h, lon_h,
    got_i, got_w, adj_i, adj_w, smem_i, smem_w,
    g_send, g_recv, e1_send, e1_recv, i_send, i_recv, n_send, n_recv,
    e2_send, e2_recv, lat_send, lat_recv, lon_send, lon_recv, loc_sem,
):
    recv_g = (recv_g0, recv_g1)
    recv_e2 = (recv_e20, recv_e21)
    p = lax.axis_index("panel")
    y = lax.axis_index("lat")
    b = lax.axis_index("lon")
    z = b // 4
    w = b % 4
    other = 1 - p
    wx = (w + 2) % 4
    me_k = y * 4 + w
    upper = y >= 2
    par = jnp.where(upper, 3 - y, y)
    dest_lat = jnp.where(upper, 3, 0)
    has_idx = (z % 2) == par
    is_ns = (y == 0) | (y == 3)
    is_agg = (w == 0) | (w == 3)
    ew_lon = jnp.where(w == 0, 0, N_LON - 1)
    is_ew = (b == 0) | (b == N_LON - 1)
    ew_side = jnp.where(b == 0, 0, 1)
    parity = z % 2
    star = jnp.where(y == 0, parity, 3 - parity)

    bar = pltpu.get_barrier_semaphore()

    def greet(dev):
        pl.semaphore_signal(bar, inc=1, device_id=dev, device_id_type=MESH)

    @pl.loop(0, 16)
    def _(k):
        @pl.when(k != me_k)
        def _():
            greet((p, k // 4, z * 4 + k % 4))

        @pl.when(is_agg)
        def _():
            greet((other, k // 4, z * 4 + k % 4))

    @pl.loop(0, 4)
    def _(m):
        greet((other, y, (2 * m + par) * 4 + wx))

    @pl.loop(0, N_Z)
    def _(zz):
        @pl.when(is_ns)
        def _():
            greet((other, star, zz * 4 + wx))

        @pl.when(is_ew & (zz != z))
        def _():
            greet((p, y, zz * 4 + w))

    @pl.when(y > 0)
    def _():
        greet((p, y - 1, b))

    @pl.when(y < N_LAT - 1)
    def _():
        greet((p, y + 1, b))

    @pl.when(b > 0)
    def _():
        greet((p, y, b - 1))

    @pl.when(b < N_LON - 1)
    def _():
        greet((p, y, b + 1))

    one = lambda cond: jnp.where(cond, 1, 0)
    peers = (
        15 + 8 + 4
        + 8 * one(has_idx)
        + one(is_agg & jnp.logical_not(is_ew))
        + one(y > 0) + one(y < N_LAT - 1) + one(b > 0) + one(b < N_LON - 1)
    )

    zero_rows = jnp.zeros((2, LON_DEV) + TILE, jnp.float32)
    for ref in (q_init, q_mid, p_lat):
        ref[0:2] = zero_rows
        ref[LAT_DEV + 2:LAT_DEV + 4] = zero_rows

    @pl.loop(0, LAT_DEV // 8)
    def _(ib):
        i0 = pl.multiple_of(ib * 8, 8)
        for j in range(LON_DEV):
            v = x_ref[:, pl.ds(i0, 8), j * NR:(j + 1) * NR]
            q_init[pl.ds(i0 + 2, 8), j] = jnp.swapaxes(v, 0, 1)

    pl.semaphore_wait(bar, peers)

    def rcopy(src, dst, ssem, rsem, dev):
        pltpu.make_async_remote_copy(
            src_ref=src, dst_ref=dst, send_sem=ssem, recv_sem=rsem,
            device_id=dev, device_id_type=MESH,
        ).start()

    def wait_on(ref, sem):
        pltpu.make_async_copy(ref, ref, sem).wait()

    @pl.when(has_idx)
    def _():
        side = jnp.where(upper, 1, 0)

        @pl.loop(0, N_Z)
        def _(zz):
            dev = (other, y, zz * 4 + wx)
            rcopy(nsi_ref.at[side], got_i.at[z // 2], i_send.at[0, zz], i_recv.at[0, z // 2], dev)
            rcopy(nsw_ref.at[side], got_w.at[z // 2], i_send.at[1, zz], i_recv.at[1, z // 2], dev)

    radius = inner_radius + (1.0 - inner_radius) * (
        lax.broadcasted_iota(jnp.int32, TILE, 1).astype(jnp.float32) + 0.5) / NR
    ct = inner_radius / radius
    ct2 = ct * ct * (viscosity / 12.0)

    def build_lhs():
        r64 = lax.broadcasted_iota(jnp.int32, (64, 8), 0) % 8
        c8 = lax.broadcasted_iota(jnp.int32, (64, 8), 1)
        ex = jnp.where(r64 == c8, 1.0, 0.0).astype(jnp.float32)
        r8 = lax.broadcasted_iota(jnp.int32, (8, 64), 0)
        c64 = lax.broadcasted_iota(jnp.int32, (8, 64), 1) % 8
        ext = jnp.where(r8 == c64, 1.0, 0.0).astype(jnp.float32)
        rr = lax.broadcasted_iota(jnp.int32, (64, 64), 0)
        cc = lax.broadcasted_iota(jnp.int32, (64, 64), 1)
        same = (rr // 8) == (cc // 8)
        eye = jnp.where(rr == cc, 1.0, 0.0).astype(jnp.float32)

        def kron(k):
            tall = jnp.dot(ex, coup_ref[k], precision=lax.Precision.HIGHEST,
                           preferred_element_type=jnp.float32)
            full = jnp.dot(tall, ext, precision=lax.Precision.HIGHEST,
                           preferred_element_type=jnp.float32)
            return jnp.where(same, full, 0.0)

        c0, c1, c2, c3 = kron(0), kron(1), kron(2), kron(3)
        nu = viscosity
        blocks = [
            (8.0 * c0 + 16.0 * nu * eye) / 12.0,
            (-8.0 * c0 + 16.0 * nu * eye) / 12.0,
            (-c0 - nu * eye) / 12.0,
            (c0 - nu * eye) / 12.0,
            c3 - (30.0 * nu / 12.0) * eye,
            c1 / -12.0,
            c2 / -12.0,
        ]
        for n, blk in enumerate(blocks):
            hi = blk.astype(jnp.bfloat16)
            lo = (blk - hi.astype(jnp.float32)).astype(jnp.bfloat16)
            lhs_ref[64 * n:64 * (n + 1), :] = jnp.concatenate([hi, hi, lo], axis=1)

    def split(cols):
        n = cols.shape[0] // 8
        flat = cols.reshape(n * 64, NR)
        wide = jnp.concatenate([flat[64 * t:64 * (t + 1)] for t in range(n)], axis=1)
        hi = wide.astype(jnp.bfloat16)
        lo = (wide - hi.astype(jnp.float32)).astype(jnp.bfloat16)
        return jnp.concatenate([hi, lo, hi], axis=0)

    def mixed(rows, cols):
        return jnp.dot(lhs_ref[rows], split(cols), preferred_element_type=jnp.float32)

    def unsplit(wide, n):
        return jnp.concatenate(
            [wide[:, NR * t:NR * (t + 1)] for t in range(n)], axis=0).reshape((8 * n,) + TILE)

    lane = lax.broadcasted_iota(jnp.int32, (64, NR), 1)

    def column(cur, idx):
        i = (idx * 43691) >> 19
        return cur[i + 2, idx - 12 * i]

    def donors(st, cur):
        @pl.loop(0, 16)
        def _(n):
            k = lax.rem(me_k + 1 + n, 16)
            ky = k // 4
            kw = k % 4
            kup = ky >= 2
            kpar = jnp.where(kup, 3 - ky, ky)
            first = (jnp.where(kup, 96, 0) + kpar * 4 + (kw + 2) % 4) * 4
            for m in range(4):
                for s in range(4):
                    send_g[st, k, m * 4 + s] = column(cur, exp_ref[first + m * 32 + s])

            @pl.when(k != me_k)
            def _():
                rcopy(send_g.at[st, k], recv_g[st].at[me_k], g_send.at[st, k],
                      g_recv.at[st, me_k], (p, ky, z * 4 + kw))

            @pl.when(k == me_k)
            def _():
                pltpu.make_async_copy(
                    send_g.at[st, k], recv_g[st].at[me_k], g_recv.at[st, me_k]).start()

        @pl.loop(0, 8)
        def _(t):
            ta = t // 2
            side = t % 2
            first = (ta * N_LON + side * (N_LON - 1)) * 4
            for s in range(4):
                send_e[st, t, s] = column(cur, exp_ref[first + s])
            rcopy(send_e.at[st, t], recv_e1.at[st, me_k], e1_send.at[st, t],
                  e1_recv.at[st, me_k], (other, ta, z * 4 + side * 3))

    def halos(st, cur):
        @pl.when(b < N_LON - 1)
        def _():
            rcopy(cur.at[2:LAT_DEV + 2, 10:12], lon_h.at[st, 0], lon_send.at[st, 0],
                  lon_recv.at[st, 0], (p, y, b + 1))

        @pl.when(b > 0)
        def _():
            rcopy(cur.at[2:LAT_DEV + 2, 0:2], lon_h.at[st, 1], lon_send.at[st, 1],
                  lon_recv.at[st, 1], (p, y, b - 1))

        @pl.when(y < N_LAT - 1)
        def _():
            rcopy(cur.at[LAT_DEV:LAT_DEV + 2], lat_h.at[st, 0], lat_send.at[st, 0],
                  lat_recv.at[st, 0], (p, y + 1, b))

        @pl.when(y > 0)
        def _():
            rcopy(cur.at[2:4], lat_h.at[st, 1], lat_send.at[st, 1],
                  lat_recv.at[st, 1], (p, y - 1, b))

    def products(cur):
        @pl.loop(0, LAT_DEV // 4)
        def _(c):
            i0 = c * 4
            cols = cur[pl.ds(i0 + 2, 4)].reshape((48,) + TILE)
            sums, lats, lons = [], [], []
            for t in range(3):
                wide = mixed(slice(0, 448), cols[16 * t:16 * (t + 1)])
                for h in range(2):
                    part = wide[:, NR * h:NR * (h + 1)]
                    total = part[256:320]
                    total = total + jnp.where(lane >= 1, pltpu.roll(part[0:64], 1, 1), 0.0)
                    total = total + jnp.where(lane < NR - 1, pltpu.roll(part[64:128], NR - 1, 1), 0.0)
                    total = total + jnp.where(lane >= 2, pltpu.roll(part[128:192], 2, 1), 0.0)
                    total = total + jnp.where(lane < NR - 2, pltpu.roll(part[192:256], NR - 2, 1), 0.0)
                    sums.append(total)
                    lats.append(part[320:384])
                    lons.append(part[384:448])
            shape = (4, LON_DEV) + TILE
            s_ref[pl.ds(i0, 4)] = jnp.concatenate(sums, axis=0).reshape(shape)
            p_lat[pl.ds(i0 + 2, 4)] = jnp.concatenate(lats, axis=0).reshape(shape)
            p_lon[pl.ds(i0, 4)] = jnp.concatenate(lons, axis=0).reshape(shape)

    def shifted(v, n):
        pad = jnp.zeros((abs(n),) + TILE, jnp.float32)
        if n > 0:
            return jnp.concatenate([v[n:], pad], axis=0)
        return jnp.concatenate([pad, v[:n]], axis=0)

    def stencil(st, cur):
        @pl.loop(0, LAT_DEV)
        def _(i):
            si = isin_ref[y * LAT_DEV + i]
            q0 = cur[i + 2]
            pl0 = p_lon[i]
            d1 = (p_lat[i] - p_lat[i + 4]) + 8.0 * (p_lat[i + 3] - p_lat[i + 1])
            e1 = (shifted(pl0, -2) - shifted(pl0, 2)) + 8.0 * (shifted(pl0, 1) - shifted(pl0, -1))
            d2 = 16.0 * (cur[i + 1] + cur[i + 3]) - (cur[i] + cur[i + 4])
            e2 = 16.0 * (shifted(q0, -1) + shifted(q0, 1)) - (shifted(q0, -2) + shifted(q0, 2))
            rate = s_ref[i] + ct * (d1 + si * e1) + ct2 * (
                d2 + (si * si) * e2 - (30.0 * (1.0 + si * si)) * q0)
            if st == 0:
                q_mid[i + 2] = q0 + time_step * rate
            else:
                res_ref[i] = 0.5 * q_init[i + 2] + 0.5 * (q0 + time_step * rate)

    def aggregate(st):
        @pl.loop(0, 16)
        def _(k):
            wait_on(recv_g[st].at[k], g_recv.at[st, k])

        @pl.loop(0, 4)
        def _(m):
            @pl.loop(0, 24)
            def _(cell):
                acc = jnp.zeros(TILE, jnp.float32)
                for t in range(4):
                    e = cell * 4 + t
                    idx = smem_i[m, 0, e]
                    acc = acc + smem_w[m, 0, e] * recv_g[st][idx >> 4, idx & 15]
                chunk[st, m, cell] = acc

            rcopy(chunk.at[st, m], recv_n.at[st, z], n_send.at[st, m], n_recv.at[st, z],
                  (other, dest_lat, (2 * m + par) * 4 + wx))

    def forward_ew(st):
        @pl.when(is_agg)
        def _():
            @pl.loop(0, 16)
            def _(k):
                wait_on(recv_e1.at[st, k], e1_recv.at[st, k])

            @pl.when(jnp.logical_not(is_ew))
            def _():
                rcopy(recv_e1.at[st], recv_e2[st].at[z], e2_send.at[st], e2_recv.at[st, z],
                      (p, y, ew_lon))

            @pl.when(is_ew)
            def _():
                pltpu.make_async_copy(recv_e1.at[st], recv_e2[st].at[z], e2_recv.at[st, z]).start()

    def adjust_indices():
        for m in range(4):
            wait_on(got_i.at[m], i_recv.at[0, m])
            wait_on(got_w.at[m], i_recv.at[1, m])
            s = got_i[m]
            col = (s >> 2) & (N_LON - 1)
            k = (s >> 7) * 4 + (col & 3)
            adj_i[m] = k * 16 + m * 4 + (s & 3)
            adj_w[m] = jnp.where((col >> 2) == z, got_w[m], 0.0)
        ci = pltpu.make_async_copy(adj_i, smem_i, loc_sem.at[0])
        cw = pltpu.make_async_copy(adj_w, smem_w, loc_sem.at[1])
        ci.start()
        cw.start()
        ci.wait()
        cw.wait()

    def border_ns(st):
        @pl.when(is_ns)
        def _():
            @pl.loop(0, N_Z)
            def _(zz):
                wait_on(recv_n.at[st, zz], n_recv.at[st, zz])

            side = jnp.where(upper, 1, 0)

            @pl.loop(0, 2)
            def _(g):
                acc = recv_n[st, 0, pl.ds(g * 12, 12)]
                for zz in range(1, N_Z):
                    acc = acc + recv_n[st, zz, pl.ds(g * 12, 12)]
                lat_h[st, side, g] = acc

    def border_ew(st):
        @pl.when(is_ew)
        def _():
            @pl.loop(0, N_Z)
            def _(zz):
                wait_on(recv_e2[st].at[zz], e2_recv.at[st, zz])

            @pl.loop(0, LAT_DEV)
            def _(i):
                for g in range(2):
                    acc = jnp.zeros(TILE, jnp.float32)
                    for t in range(4):
                        e = ew_side * 512 + i * 8 + g * 4 + t
                        s = ewi_ref[e]
                        col = (s >> 2) & (N_LON - 1)
                        k = (s >> 7) * 4 + (col & 3)
                        acc = acc + eww_ref[e] * recv_e2[st][col >> 2, k, s & 3]
                    lon_h[st, ew_side, i, g] = acc

    def wait_halos(st):
        @pl.when(b > 0)
        def _():
            wait_on(lon_h.at[st, 0], lon_recv.at[st, 0])

        @pl.when(b < N_LON - 1)
        def _():
            wait_on(lon_h.at[st, 1], lon_recv.at[st, 1])

        @pl.when(y > 0)
        def _():
            wait_on(lat_h.at[st, 0], lat_recv.at[st, 0])

        @pl.when(y < N_LAT - 1)
        def _():
            wait_on(lat_h.at[st, 1], lat_recv.at[st, 1])

    def correct(st):
        if st == 0:
            dst, off, scale = q_mid, 2, time_step
        else:
            dst, off, scale = res_ref, 0, 0.5 * time_step
        hal = lat_h[st].reshape((48,) + TILE)
        mix_lat = jnp.concatenate(
            [unsplit(mixed(slice(320, 384), hal[16 * t:16 * (t + 1)]), 2) for t in range(3)],
            axis=0).reshape((2, 2, LON_DEV) + TILE)
        hal = hal.reshape((2, 2, LON_DEV) + TILE)
        sc, sc2 = scale * ct, scale * ct2
        dst[off] += sc * (mix_lat[0, 0] - 8.0 * mix_lat[0, 1]) + sc2 * (16.0 * hal[0, 1] - hal[0, 0])
        dst[off + 1] += sc * mix_lat[0, 1] - sc2 * hal[0, 1]
        dst[off + 63] += sc * (8.0 * mix_lat[1, 0] - mix_lat[1, 1]) + sc2 * (16.0 * hal[1, 0] - hal[1, 1])
        dst[off + 62] += -sc * mix_lat[1, 0] - sc2 * hal[1, 0]

        @pl.loop(0, LAT_DEV // 4)
        def _(c):
            i0 = c * 4
            west = lon_h[st, 0, pl.ds(i0, 4)].reshape((8,) + TILE)
            east = lon_h[st, 1, pl.ds(i0, 4)].reshape((8,) + TILE)
            both = unsplit(mixed(slice(384, 448), jnp.concatenate([west, east], axis=0)), 2)
            for n in range(4):
                i = i0 + n
                si = isin_ref[y * LAT_DEV + i]
                a1 = sc * si
                a2 = sc2 * (si * si)
                w2, w1, pw2, pw1 = west[2 * n], west[2 * n + 1], both[2 * n], both[2 * n + 1]
                e1, e2, pe1, pe2 = east[2 * n], east[2 * n + 1], both[8 + 2 * n], both[9 + 2 * n]
                dst[off + i, 0] += a1 * (pw2 - 8.0 * pw1) + a2 * (16.0 * w1 - w2)
                dst[off + i, 1] += a1 * pw1 - a2 * w1
                dst[off + i, 11] += a1 * (8.0 * pe1 - pe2) + a2 * (16.0 * e1 - e2)
                dst[off + i, 10] += -a1 * pe1 - a2 * e1

    for st, cur in ((0, q_init), (1, q_mid)):
        donors(st, cur)
        halos(st, cur)
        if st == 0:
            build_lhs()
            adjust_indices()
        products(cur)
        forward_ew(st)
        aggregate(st)
        stencil(st, cur)
        wait_halos(st)
        border_ns(st)
        border_ew(st)
        correct(st)

    @pl.loop(0, LAT_DEV // 8)
    def _(ib):
        i0 = pl.multiple_of(ib * 8, 8)
        for j in range(LON_DEV):
            v = res_ref[pl.ds(i0, 8), j]
            out_ref[:, pl.ds(i0, 8), j * NR:(j + 1) * NR] = jnp.swapaxes(v, 0, 1)

    @pl.when(has_idx)
    def _():
        @pl.loop(0, N_Z)
        def _(zz):
            wait_on(nsi_ref.at[0], i_send.at[0, zz])
            wait_on(nsw_ref.at[0], i_send.at[1, zz])

    for st, cur in ((0, q_init), (1, q_mid)):
        @pl.loop(0, 16)
        def _(k):
            @pl.when(k != me_k)
            def _():
                wait_on(send_g.at[st, k], g_send.at[st, k])

        @pl.loop(0, 8)
        def _(t):
            wait_on(send_e.at[st, t], e1_send.at[st, t])

        @pl.loop(0, 4)
        def _(m):
            wait_on(chunk.at[st, m], n_send.at[st, m])

        @pl.when(is_agg & jnp.logical_not(is_ew))
        def _():
            wait_on(recv_e1.at[st], e2_send.at[st])

        @pl.when(b < N_LON - 1)
        def _():
            wait_on(lon_h.at[st, 0], lon_send.at[st, 0])

        @pl.when(b > 0)
        def _():
            wait_on(lon_h.at[st, 1], lon_send.at[st, 1])

        @pl.when(y < N_LAT - 1)
        def _():
            wait_on(lat_h.at[st, 0], lat_send.at[st, 0])

        @pl.when(y > 0)
        def _():
            wait_on(lat_h.at[st, 1], lat_send.at[st, 1])


def corner_weights(frac):
    a, c = frac[..., 0], frac[..., 1]
    return jnp.stack(
        [(1.0 - a) * (1.0 - c), a * (1.0 - c), (1.0 - a) * c, a * c], axis=-1)


def inverse_sines():
    total = LAT_DEV * N_LAT
    colat = math.pi / 4 + (jnp.arange(total, dtype=jnp.int32).astype(jnp.float32) + 0.5) * (
        math.pi / 2) / total
    return 1.0 / jnp.sin(colat)


def local(
    fields, coupling, export_index, ghost_ns_index, ghost_ns_frac, ghost_ew_index, ghost_ew_frac
):
    x = fields[0]

    def padded(v):
        flat = jnp.pad(v.reshape(2, 1, 96), ((0, 0), (0, 7), (0, 32)))
        return flat

    nsi = padded(ghost_ns_index[0])
    nsw = padded(corner_weights(ghost_ns_frac[0]))
    exports = export_index.reshape(-1)
    ewi = ghost_ew_index.reshape(-1)
    eww = corner_weights(ghost_ew_frac[0]).reshape(-1)
    isin = inverse_sines()

    vm = pl.BlockSpec(memory_space=pltpu.VMEM)
    sm = pl.BlockSpec(memory_space=pltpu.SMEM)
    V = lambda *shape: pltpu.VMEM(shape + TILE, jnp.float32)
    D = lambda *shape: pltpu.SemaphoreType.DMA(shape)
    out = pl.pallas_call(
        kernel,
        out_shape=jax.ShapeDtypeStruct(x.shape, jnp.float32),
        in_specs=[vm, vm, vm, vm, sm, sm, sm, sm],
        out_specs=vm,
        scratch_shapes=[
            V(LAT_DEV + 4, LON_DEV), V(LAT_DEV + 4, LON_DEV), V(LAT_DEV + 4, LON_DEV),
            V(LAT_DEV, LON_DEV), V(LAT_DEV, LON_DEV), V(LAT_DEV, LON_DEV),
            pltpu.VMEM((448, 192), jnp.bfloat16),
            V(2, 16, 16), V(16, 16), V(16, 16), V(2, 8, 4), V(2, 16, 4), V(N_Z, 16, 4), V(N_Z, 16, 4),
            V(2, 4, 24), V(2, N_Z, 24), V(2, 2, 2, LON_DEV), V(2, 2, LAT_DEV, 2),
            pltpu.VMEM((4,) + TILE, jnp.int32), V(4),
            pltpu.VMEM((4,) + TILE, jnp.int32), V(4),
            pltpu.SMEM((4,) + TILE, jnp.int32), pltpu.SMEM((4,) + TILE, jnp.float32),
            D(2, 16), D(2, 16), D(2, 8), D(2, 16), D(2, 8), D(2, 4), D(2, 4), D(2, N_Z),
            D(2), D(2, N_Z), D(2, 2), D(2, 2), D(2, 2), D(2, 2), D(2),
        ],
        compiler_params=pltpu.CompilerParams(
            collective_id=0, has_side_effects=True, vmem_limit_bytes=60 * 2**20),
        name="two_sections",
    )(x, coupling, nsi, nsw, exports, ewi, eww, isin)
    return out[None]


def solution(mesh):
    placed = (
        P("panel", None, "lat", "lon"),
        P(),
        P("panel", "lat", "lon", None),
        P("panel", None, None, "lon", None),
        P("panel", None, None, "lon", None),
        P("panel", None, "lat", None, None),
        P("panel", None, "lat", None, None),
    )
    return jax.shard_map(
        local, mesh=mesh, in_specs=placed, out_specs=P("panel", None, "lat", "lon"), check_vma=False
    )
```

profile of v0, /device:TPU:28, one launch (start us, length us, event | category | flops | bytes accessed | tf_op | source)
XLA Modules:
  0.0 117.2 jit_solution(203408536156967384)
XLA Ops:
  0.0 0.6 sine_divide_fusion.isin_ref
  0.6 0.8 subtract_multiply_fusion.4
  1.4 0.8 subtract_multiply_fusion.1
  2.2 0.1 copy.12
  2.3 0.1 reshape.12
  2.4 0.6 pad.9.nsw_ref
  3.0 0.8 copy.10
  3.8 0.1 reshape_squeeze.3
  3.9 0.6 pad.8.nsi_ref
  4.5 0.1 copy.15
  4.7 0.8 reshape.15.eww_ref
  5.5 0.8 copy.14
  6.3 0.8 reshape.14.ewi_ref
  7.1 106.3 %two_sections.1 = f32[8,64,1536]{2,1,0:T(8,128)} custom-call(f32[8,64,1536]{2,1,0:T(8,128)} %bitcast.8, f32[4,8,8]{2,1,0:T(8,128)} %coup_ref.1, s32[2,8,128]{2,1,0:T(8,128)} %pad.8.nsi_ref, f32[2,8,128]{2,1,0:T(8,128)} %pad.9.nsw_ref, s32[512]{0:T(512)} %bitcast.13, s32[1024]{0:T(1024)} %reshape.14.ewi_ref, f32[1024]{0:T(1024)} %reshape.15.eww_ref, ...), custom_call_target="tpu_custom_call" | custom-call | tf_op jit(solution)/shard_map/two_sections/pallas_call | solution.py:540
  113.4 3.8 %copy.17 = f32[1,8,64,1536]{3,2,1,0:T(8,128)} copy(f32[1,8,64,1536]{3,2,1,0:T(8,128)} %bitcast.7) | data formatting | bytes 6291456
  (2 shorter events, 0.0 us)
where the time goes:
time: 117 us
  Pallas kernels  106 us (91%)
  local copies, waits for them, and re-layouts  8.62 us (7%)
  other arithmetic  2.2 us (2%)
    pallas_call x1, Pallas kernels, local(): pl.pallas_call(kernel, out_shape=jax.ShapeDtypeStruct(x.shape, jnp.float3...  106 us
    unnamed x3, local copies, waits for them, and re-layouts  5.38 us

commit v1 on v0

v1 whole, which is shorter than its diff:
```python
import math

import jax
import jax.numpy as jnp
from jax import lax
from jax.experimental import pallas as pl
from jax.experimental.pallas import tpu as pltpu
from jax.sharding import PartitionSpec as P

NR = 128
FIELDS = 8
LAT_DEV = 64
LON_DEV = 12
N_LAT = 4
N_LON = 32
N_Z = 8

time_step = 0.15
viscosity = 0.1
inner_radius = 0.35

MESH = pl.DeviceIdType.MESH
TILE = (FIELDS, NR)


def kernel(
    x_ref, coup_ref, nsi_ref, nsf_ref, exp_ref, ewi_ref, ewf_ref,
    out_ref,
    x_buf, q_init, q_mid, p_lat, p_lon, s_ref, res_ref, lhs_ref, isin_ref,
    send_g, recv_g0, recv_g1, send_e, recv_e1, recv_e20, recv_e21, chunk, recv_n, summed,
    lat_h, lon_h,
    own_i, own_w, got_i, got_w, adj_i, adj_w, smem_i, smem_w,
    adj_ei, adj_ew, smem_ei, smem_ew,
    g_send, g_recv, e1_send, e1_recv, i_send, i_recv, n_send, n_recv, f_send,
    e2_send, e2_recv, lat_send, lat_recv, lon_send, lon_recv, loc_sem,
):
    recv_g = (recv_g0, recv_g1)
    recv_e2 = (recv_e20, recv_e21)
    p = lax.axis_index("panel")
    y = lax.axis_index("lat")
    b = lax.axis_index("lon")
    z = b // 4
    w = b % 4
    other = 1 - p
    wx = (w + 2) % 4
    me_k = y * 4 + w
    upper = y >= 2
    half = jnp.where(upper, 1, 0)
    par = jnp.where(upper, 3 - y, y)
    dest_lat = jnp.where(upper, 3, 0)
    is_sum = (z % 2) == par
    is_ns = (y == 0) | (y == 3)
    is_agg = (w == 1) | (w == 2)
    ew_lon = jnp.where(w == 2, 0, N_LON - 1)
    is_ew = (b == 0) | (b == N_LON - 1)
    ew_side = jnp.where(b == 0, 0, 1)
    star = jnp.where(y == 0, z % 2, 3 - z % 2)

    x_copy = pltpu.make_async_copy(x_ref, x_buf, loc_sem.at[0])
    x_copy.start()

    bar = pltpu.get_barrier_semaphore()

    def greet(dev):
        pl.semaphore_signal(bar, inc=1, device_id=dev, device_id_type=MESH)

    @pl.loop(0, 16)
    def _(k):
        @pl.when(k != me_k)
        def _():
            greet((p, k // 4, z * 4 + k % 4))

    @pl.loop(0, 4)
    def _(m):
        greet((other, y, (2 * m + par) * 4 + wx))

    @pl.loop(0, N_Z)
    def _(zz):
        @pl.when(is_sum & (zz != z))
        def _():
            greet((p, y, zz * 4 + w))

        @pl.when(is_ew)
        def _():
            greet((other, y, zz * 4 + wx))

    @pl.when(is_ns)
    def _():
        greet((other, star, z * 4 + wx))

    @pl.when(y > 0)
    def _():
        greet((p, y - 1, b))

    @pl.when(y < N_LAT - 1)
    def _():
        greet((p, y + 1, b))

    @pl.when(b > 0)
    def _():
        greet((p, y, b - 1))

    @pl.when(b < N_LON - 1)
    def _():
        greet((p, y, b + 1))

    one = lambda cond: jnp.where(cond, 1, 0)
    peers = (
        15 + 4 + 8 * one(is_sum) + one(is_agg)
        + one(y > 0) + one(y < N_LAT - 1) + one(b > 0) + one(b < N_LON - 1)
    )

    def rcopy(src, dst, ssem, rsem, dev):
        pltpu.make_async_remote_copy(
            src_ref=src, dst_ref=dst, send_sem=ssem, recv_sem=rsem,
            device_id=dev, device_id_type=MESH,
        ).start()

    def wait_on(ref, sem):
        pltpu.make_async_copy(ref, ref, sem).wait()

    row = lax.broadcasted_iota(jnp.int32, TILE, 0)

    def weights_of(frac):
        a, c = frac[0:1], frac[1:2]
        return jnp.where(row % 2 == 1, a, 1.0 - a) * jnp.where(row % 4 >= 2, c, 1.0 - c)

    def prepare_indices():
        own_i[...] = jnp.zeros(own_i.shape, jnp.int32)
        own_w[...] = jnp.zeros(own_w.shape, jnp.float32)
        adj_ei[...] = jnp.zeros(adj_ei.shape, jnp.int32)
        adj_ew[...] = jnp.zeros(adj_ew.shape, jnp.float32)
        for g in range(2):
            own_i[g, 0:4, 0:LON_DEV] = nsi_ref[half, g]
            own_w[g, 0:2, 0:LON_DEV] = nsf_ref[half, g]
            own_w[g] = weights_of(own_w[g])
            adj_ei[g, 0:4, 0:LAT_DEV] = ewi_ref[ew_side, g]
            adj_ew[g, 0:2, 0:LAT_DEV] = ewf_ref[ew_side, g]
            adj_ew[g] = weights_of(adj_ew[g])
            s = adj_ei[g]
            col = (s >> 2) & (N_LON - 1)
            k = (s >> 7) * 4 + (col & 3)
            adj_ei[g] = (col >> 2) * 64 + k * 4 + (s & 3)
        copies = [pltpu.make_async_copy(adj_ei, smem_ei, loc_sem.at[1]),
                  pltpu.make_async_copy(adj_ew, smem_ew, loc_sem.at[2])]
        for c in copies:
            c.start()
        for c in copies:
            c.wait()

    def send_indices():
        @pl.when(is_sum)
        def _():
            @pl.loop(0, N_Z)
            def _(zz):
                dev = (other, y, zz * 4 + wx)
                rcopy(own_i, got_i.at[z // 2], i_send.at[0, zz], i_recv.at[0, z // 2], dev)
                rcopy(own_w, got_w.at[z // 2], i_send.at[1, zz], i_recv.at[1, z // 2], dev)

    def adjust_indices():
        for m in range(4):
            wait_on(got_i.at[m], i_recv.at[0, m])
            wait_on(got_w.at[m], i_recv.at[1, m])
            s = got_i[m]
            col = (s >> 2) & (N_LON - 1)
            k = (s >> 7) * 4 + (col & 3)
            adj_i[m] = k * 16 + m * 4 + (s & 3)
            adj_w[m] = jnp.where((col >> 2) == z, got_w[m], 0.0)
        copies = [pltpu.make_async_copy(adj_i, smem_i, loc_sem.at[3]),
                  pltpu.make_async_copy(adj_w, smem_w, loc_sem.at[4])]
        for c in copies:
            c.start()
        for c in copies:
            c.wait()

    def load_state():
        zero_rows = jnp.zeros((2, LON_DEV) + TILE, jnp.float32)
        for ref in (q_init, q_mid, p_lat):
            ref[0:2] = zero_rows
            ref[LAT_DEV + 2:LAT_DEV + 4] = zero_rows
        x_copy.wait()

        @pl.loop(0, LAT_DEV // 8)
        def _(ib):
            i0 = pl.multiple_of(ib * 8, 8)
            for j in range(LON_DEV):
                v = x_buf[:, pl.ds(i0, 8), j * NR:(j + 1) * NR]
                q_init[pl.ds(i0 + 2, 8), j] = jnp.swapaxes(v, 0, 1)

    radius = inner_radius + (1.0 - inner_radius) * (
        lax.broadcasted_iota(jnp.int32, TILE, 1).astype(jnp.float32) + 0.5) / NR
    ct = inner_radius / radius
    ct2 = ct * ct * (viscosity / 12.0)

    def build_sines():
        i = y * LAT_DEV + lax.broadcasted_iota(jnp.int32, (LAT_DEV, NR), 0)
        colat = math.pi / 4 + (i.astype(jnp.float32) + 0.5) * (math.pi / 2) / (LAT_DEV * N_LAT)
        isin_ref[...] = 1.0 / jnp.sin(colat)

    def inv_sin(i):
        return isin_ref[pl.ds(i, 1), :]

    def build_lhs():
        r64 = lax.broadcasted_iota(jnp.int32, (64, 8), 0) % 8
        c8 = lax.broadcasted_iota(jnp.int32, (64, 8), 1)
        ex = jnp.where(r64 == c8, 1.0, 0.0).astype(jnp.float32)
        r8 = lax.broadcasted_iota(jnp.int32, (8, 64), 0)
        c64 = lax.broadcasted_iota(jnp.int32, (8, 64), 1) % 8
        ext = jnp.where(r8 == c64, 1.0, 0.0).astype(jnp.float32)
        rr = lax.broadcasted_iota(jnp.int32, (64, 64), 0)
        cc = lax.broadcasted_iota(jnp.int32, (64, 64), 1)
        same = (rr // 8) == (cc // 8)
        eye = jnp.where(rr == cc, 1.0, 0.0).astype(jnp.float32)

        def kron(k):
            tall = jnp.dot(ex, coup_ref[k], precision=lax.Precision.HIGHEST,
                           preferred_element_type=jnp.float32)
            full = jnp.dot(tall, ext, precision=lax.Precision.HIGHEST,
                           preferred_element_type=jnp.float32)
            return jnp.where(same, full, 0.0)

        c0, c1, c2, c3 = kron(0), kron(1), kron(2), kron(3)
        nu = viscosity
        blocks = [
            (8.0 * c0 + 16.0 * nu * eye) / 12.0,
            (-8.0 * c0 + 16.0 * nu * eye) / 12.0,
            (-c0 - nu * eye) / 12.0,
            (c0 - nu * eye) / 12.0,
            c3 - (30.0 * nu / 12.0) * eye,
            c1 / -12.0,
            c2 / -12.0,
        ]
        for n, blk in enumerate(blocks):
            hi = blk.astype(jnp.bfloat16)
            lo = (blk - hi.astype(jnp.float32)).astype(jnp.bfloat16)
            lhs_ref[64 * n:64 * (n + 1), :] = jnp.concatenate([hi, hi, lo], axis=1)

    def split(cols):
        n = cols.shape[0] // 8
        flat = cols.reshape(n * 64, NR)
        wide = jnp.concatenate([flat[64 * t:64 * (t + 1)] for t in range(n)], axis=1)
        hi = wide.astype(jnp.bfloat16)
        lo = (wide - hi.astype(jnp.float32)).astype(jnp.bfloat16)
        return jnp.concatenate([hi, lo, hi], axis=0)

    def mixed(rows, cols):
        return jnp.dot(lhs_ref[rows], split(cols), preferred_element_type=jnp.float32)

    def unsplit(wide, n):
        return jnp.concatenate(
            [wide[:, NR * t:NR * (t + 1)] for t in range(n)], axis=0).reshape((8 * n,) + TILE)

    lane = lax.broadcasted_iota(jnp.int32, (64, NR), 1)

    def column(cur, idx):
        i = (idx * 43691) >> 19
        return cur[i + 2, idx - 12 * i]

    def group_of(k):
        ky = k // 4
        kup = ky >= 2
        kpar = jnp.where(kup, 3 - ky, ky)
        return (jnp.where(kup, 96, 0) + kpar * 4 + (k % 4 + 2) % 4) * 4

    def gather_g(st, cur, k):
        first = group_of(k)
        for m in range(4):
            for s in range(4):
                send_g[st, k, m * 4 + s] = column(cur, exp_ref[first + m * 32 + s])

    def start_g(st, k):
        @pl.when(k != me_k)
        def _():
            rcopy(send_g.at[st, k], recv_g[st].at[me_k], g_send.at[st, k],
                  g_recv.at[st, me_k], (p, k // 4, z * 4 + k % 4))

        @pl.when(k == me_k)
        def _():
            pltpu.make_async_copy(
                send_g.at[st, k], recv_g[st].at[me_k], g_recv.at[st, me_k]).start()

    def gather_e(st, cur, t):
        first = ((t // 2) * N_LON + (t % 2) * (N_LON - 1)) * 4
        for s in range(4):
            send_e[st, t, s] = column(cur, exp_ref[first + s])

    def ew_member(t):
        return (t // 2) * 4 + 2 - t % 2

    def start_e(st, t):
        k = ew_member(t)

        @pl.when(k != me_k)
        def _():
            rcopy(send_e.at[st, t], recv_e1.at[st, me_k], e1_send.at[st, t],
                  e1_recv.at[st, me_k], (p, k // 4, z * 4 + k % 4))

        @pl.when(k == me_k)
        def _():
            pltpu.make_async_copy(
                send_e.at[st, t], recv_e1.at[st, me_k], e1_recv.at[st, me_k]).start()

    def turn(n):
        return lax.rem(me_k + 1 + n, 16)

    def halos(st, cur):
        @pl.when(y < N_LAT - 1)
        def _():
            rcopy(cur.at[LAT_DEV:LAT_DEV + 2], lat_h.at[st, 0], lat_send.at[st, 0],
                  lat_recv.at[st, 0], (p, y + 1, b))

        @pl.when(y > 0)
        def _():
            rcopy(cur.at[2:4], lat_h.at[st, 1], lat_send.at[st, 1],
                  lat_recv.at[st, 1], (p, y - 1, b))

        @pl.when(b < N_LON - 1)
        def _():
            rcopy(cur.at[2:LAT_DEV + 2, 10:12], lon_h.at[st, 0], lon_send.at[st, 0],
                  lon_recv.at[st, 0], (p, y, b + 1))

        @pl.when(b > 0)
        def _():
            rcopy(cur.at[2:LAT_DEV + 2, 0:2], lon_h.at[st, 1], lon_send.at[st, 1],
                  lon_recv.at[st, 1], (p, y, b - 1))

    def products(cur):
        @pl.loop(0, LAT_DEV // 4)
        def _(c):
            i0 = c * 4
            cols = cur[pl.ds(i0 + 2, 4)].reshape((48,) + TILE)
            sums, lats, lons = [], [], []
            for t in range(3):
                wide = mixed(slice(0, 448), cols[16 * t:16 * (t + 1)])
                for h in range(2):
                    part = wide[:, NR * h:NR * (h + 1)]
                    total = part[256:320]
                    total = total + jnp.where(lane >= 1, pltpu.roll(part[0:64], 1, 1), 0.0)
                    total = total + jnp.where(lane < NR - 1, pltpu.roll(part[64:128], NR - 1, 1), 0.0)
                    total = total + jnp.where(lane >= 2, pltpu.roll(part[128:192], 2, 1), 0.0)
                    total = total + jnp.where(lane < NR - 2, pltpu.roll(part[192:256], NR - 2, 1), 0.0)
                    sums.append(total)
                    lats.append(part[320:384])
                    lons.append(part[384:448])
            shape = (4, LON_DEV) + TILE
            s_ref[pl.ds(i0, 4)] = jnp.concatenate(sums, axis=0).reshape(shape)
            p_lat[pl.ds(i0 + 2, 4)] = jnp.concatenate(lats, axis=0).reshape(shape)
            p_lon[pl.ds(i0, 4)] = jnp.concatenate(lons, axis=0).reshape(shape)

    def shifted(v, n):
        pad = jnp.zeros((abs(n),) + TILE, jnp.float32)
        if n > 0:
            return jnp.concatenate([v[n:], pad], axis=0)
        return jnp.concatenate([pad, v[:n]], axis=0)

    def stencil(st, cur):
        @pl.loop(0, LAT_DEV)
        def _(i):
            si = inv_sin(i)
            q0 = cur[i + 2]
            pl0 = p_lon[i]
            d1 = (p_lat[i] - p_lat[i + 4]) + 8.0 * (p_lat[i + 3] - p_lat[i + 1])
            e1 = (shifted(pl0, -2) - shifted(pl0, 2)) + 8.0 * (shifted(pl0, 1) - shifted(pl0, -1))
            d2 = 16.0 * (cur[i + 1] + cur[i + 3]) - (cur[i] + cur[i + 4])
            e2 = 16.0 * (shifted(q0, -1) + shifted(q0, 1)) - (shifted(q0, -2) + shifted(q0, 2))
            rate = s_ref[i] + ct * (d1 + si * e1) + ct2 * (
                d2 + (si * si) * e2 - (30.0 * (1.0 + si * si)) * q0)
            if st == 0:
                q_mid[i + 2] = q0 + time_step * rate
            else:
                res_ref[i] = 0.5 * q_init[i + 2] + 0.5 * (q0 + time_step * rate)

    def aggregate(st):
        @pl.loop(0, 16)
        def _(k):
            wait_on(recv_g[st].at[k], g_recv.at[st, k])

        @pl.loop(0, 4)
        def _(m):
            @pl.loop(0, LON_DEV)
            def _(j):
                for g in range(2):
                    acc = jnp.zeros(TILE, jnp.float32)
                    for t in range(4):
                        idx = smem_i[m, g, t, j]
                        acc = acc + smem_w[m, g, t, j] * recv_g[st][idx >> 4, idx & 15]
                    chunk[st, m, g, j] = acc

            zz = 2 * m + par

            @pl.when(zz != z)
            def _():
                rcopy(chunk.at[st, m], recv_n.at[st, z], n_send.at[st, m], n_recv.at[st, z],
                      (p, y, zz * 4 + w))

            @pl.when(zz == z)
            def _():
                pltpu.make_async_copy(chunk.at[st, m], recv_n.at[st, z], n_recv.at[st, z]).start()

    def sum_over_z(st):
        @pl.when(is_sum)
        def _():
            @pl.loop(0, N_Z)
            def _(zz):
                wait_on(recv_n.at[st, zz], n_recv.at[st, zz])

            for g in range(2):
                acc = recv_n[st, 0, g]
                for zz in range(1, N_Z):
                    acc = acc + recv_n[st, zz, g]
                summed[st, g] = acc
            rcopy(summed.at[st], lat_h.at[st, half], f_send.at[st], lat_recv.at[st, half],
                  (other, dest_lat, z * 4 + wx))

    def forward_ew(st):
        @pl.when(is_agg)
        def _():
            @pl.loop(0, 16)
            def _(k):
                wait_on(recv_e1.at[st, k], e1_recv.at[st, k])

            rcopy(recv_e1.at[st], recv_e2[st].at[z], e2_send.at[st], e2_recv.at[st, z],
                  (other, y, ew_lon))

    def border_ew(st):
        @pl.when(is_ew)
        def _():
            @pl.loop(0, N_Z)
            def _(zz):
                wait_on(recv_e2[st].at[zz], e2_recv.at[st, zz])

            @pl.loop(0, LAT_DEV)
            def _(i):
                for g in range(2):
                    acc = jnp.zeros(TILE, jnp.float32)
                    for t in range(4):
                        idx = smem_ei[g, t, i]
                        acc = acc + smem_ew[g, t, i] * recv_e2[st][idx >> 6, (idx >> 2) & 15, idx & 3]
                    lon_h[st, ew_side, i, g] = acc

    def wait_lon(st):
        @pl.when(b > 0)
        def _():
            wait_on(lon_h.at[st, 0], lon_recv.at[st, 0])

        @pl.when(b < N_LON - 1)
        def _():
            wait_on(lon_h.at[st, 1], lon_recv.at[st, 1])

    def wait_lat(st):
        for side in range(2):
            wait_on(lat_h.at[st, side], lat_recv.at[st, side])

    def target(st):
        if st == 0:
            return q_mid, 2, time_step * ct, time_step * ct2
        return res_ref, 0, 0.5 * time_step * ct, 0.5 * time_step * ct2

    def correct_lat(st):
        dst, off, sc, sc2 = target(st)
        hal = lat_h[st].reshape((48,) + TILE)
        mix_lat = jnp.concatenate(
            [unsplit(mixed(slice(320, 384), hal[16 * t:16 * (t + 1)]), 2) for t in range(3)],
            axis=0).reshape((2, 2, LON_DEV) + TILE)
        hal = hal.reshape((2, 2, LON_DEV) + TILE)
        dst[off] += sc * (mix_lat[0, 0] - 8.0 * mix_lat[0, 1]) + sc2 * (16.0 * hal[0, 1] - hal[0, 0])
        dst[off + 1] += sc * mix_lat[0, 1] - sc2 * hal[0, 1]
        dst[off + 63] += sc * (8.0 * mix_lat[1, 0] - mix_lat[1, 1]) + sc2 * (16.0 * hal[1, 0] - hal[1, 1])
        dst[off + 62] += -sc * mix_lat[1, 0] - sc2 * hal[1, 0]

    def correct_lon(st):
        dst, off, sc, sc2 = target(st)

        @pl.loop(0, LAT_DEV // 4)
        def _(c):
            i0 = c * 4
            west = lon_h[st, 0, pl.ds(i0, 4)].reshape((8,) + TILE)
            east = lon_h[st, 1, pl.ds(i0, 4)].reshape((8,) + TILE)
            both = unsplit(mixed(slice(384, 448), jnp.concatenate([west, east], axis=0)), 2)
            for n in range(4):
                i = i0 + n
                si = inv_sin(i)
                a1 = sc * si
                a2 = sc2 * (si * si)
                w2, w1, pw2, pw1 = west[2 * n], west[2 * n + 1], both[2 * n], both[2 * n + 1]
                e1, e2, pe1, pe2 = east[2 * n], east[2 * n + 1], both[8 + 2 * n], both[9 + 2 * n]
                dst[off + i, 0] += a1 * (pw2 - 8.0 * pw1) + a2 * (16.0 * w1 - w2)
                dst[off + i, 1] += a1 * pw1 - a2 * w1
                dst[off + i, 11] += a1 * (8.0 * pe1 - pe2) + a2 * (16.0 * e1 - e2)
                dst[off + i, 10] += -a1 * pe1 - a2 * e1

    load_state()

    @pl.loop(0, 8)
    def _(t):
        gather_e(0, q_init, t)

    @pl.loop(0, 16)
    def _(n):
        gather_g(0, q_init, n)

    prepare_indices()
    build_lhs()
    build_sines()
    pl.semaphore_wait(bar, peers)

    for st, cur in ((0, q_init), (1, q_mid)):
        @pl.loop(0, 8)
        def _(t):
            if st == 1:
                gather_e(st, cur, t)
            start_e(st, t)

        if st == 0:
            send_indices()

        @pl.loop(0, 16)
        def _(n):
            k = turn(n)
            if st == 1:
                gather_g(st, cur, k)
            start_g(st, k)

        if st == 0:
            adjust_indices()
        forward_ew(st)
        products(cur)
        aggregate(st)
        halos(st, cur)
        stencil(st, cur)
        sum_over_z(st)
        wait_lon(st)
        border_ew(st)
        correct_lon(st)
        wait_lat(st)
        correct_lat(st)

    @pl.loop(0, LAT_DEV // 8)
    def _(ib):
        i0 = pl.multiple_of(ib * 8, 8)
        for j in range(LON_DEV):
            v = res_ref[pl.ds(i0, 8), j]
            out_ref[:, pl.ds(i0, 8), j * NR:(j + 1) * NR] = jnp.swapaxes(v, 0, 1)

    @pl.when(is_sum)
    def _():
        @pl.loop(0, N_Z)
        def _(zz):
            wait_on(own_i, i_send.at[0, zz])
            wait_on(own_w, i_send.at[1, zz])

    for st in range(2):
        @pl.loop(0, 16)
        def _(k):
            @pl.when(k != me_k)
            def _():
                wait_on(send_g.at[st, k], g_send.at[st, k])

        @pl.loop(0, 8)
        def _(t):
            @pl.when(ew_member(t) != me_k)
            def _():
                wait_on(send_e.at[st, t], e1_send.at[st, t])

        @pl.loop(0, 4)
        def _(m):
            @pl.when(2 * m + par != z)
            def _():
                wait_on(chunk.at[st, m], n_send.at[st, m])

        @pl.when(is_sum)
        def _():
            wait_on(summed.at[st], f_send.at[st])

        @pl.when(is_agg)
        def _():
            wait_on(recv_e1.at[st], e2_send.at[st])

        @pl.when(b < N_LON - 1)
        def _():
            wait_on(lon_h.at[st, 0], lon_send.at[st, 0])

        @pl.when(b > 0)
        def _():
            wait_on(lon_h.at[st, 1], lon_send.at[st, 1])

        @pl.when(y < N_LAT - 1)
        def _():
            wait_on(lat_h.at[st, 0], lat_send.at[st, 0])

        @pl.when(y > 0)
        def _():
            wait_on(lat_h.at[st, 1], lat_send.at[st, 1])


def local(
    fields, coupling, export_index, ghost_ns_index, ghost_ns_frac, ghost_ew_index, ghost_ew_frac
):
    x = fields[0]
    exports = export_index.reshape(-1)
    nsi = jnp.swapaxes(ghost_ns_index[0], 2, 3)
    nsf = jnp.swapaxes(ghost_ns_frac[0], 2, 3)
    ewi = jnp.transpose(ghost_ew_index[0], (0, 2, 3, 1))
    ewf = jnp.transpose(ghost_ew_frac[0], (0, 2, 3, 1))

    vm = pl.BlockSpec(memory_space=pltpu.VMEM)
    sm = pl.BlockSpec(memory_space=pltpu.SMEM)
    hbm = pl.BlockSpec(memory_space=pl.ANY)
    V = lambda *shape: pltpu.VMEM(shape + TILE, jnp.float32)
    I = lambda *shape: pltpu.VMEM(shape + TILE, jnp.int32)
    D = lambda *shape: pltpu.SemaphoreType.DMA(shape)
    out = pl.pallas_call(
        kernel,
        out_shape=jax.ShapeDtypeStruct(x.shape, jnp.float32),
        in_specs=[hbm, vm, vm, vm, sm, vm, vm],
        out_specs=vm,
        scratch_shapes=[
            pltpu.VMEM(x.shape, jnp.float32),
            V(LAT_DEV + 4, LON_DEV), V(LAT_DEV + 4, LON_DEV), V(LAT_DEV + 4, LON_DEV),
            V(LAT_DEV, LON_DEV), V(LAT_DEV, LON_DEV), V(LAT_DEV, LON_DEV),
            pltpu.VMEM((448, 192), jnp.bfloat16), pltpu.VMEM((LAT_DEV, NR), jnp.float32),
            V(2, 16, 16), V(16, 16), V(16, 16), V(2, 8, 4), V(2, 16, 4), V(N_Z, 16, 4), V(N_Z, 16, 4),
            V(2, 4, 2, LON_DEV), V(2, N_Z, 2, LON_DEV), V(2, 2, LON_DEV),
            V(2, 2, 2, LON_DEV), V(2, 2, LAT_DEV, 2),
            I(2), V(2), I(4, 2), V(4, 2), I(4, 2), V(4, 2),
            pltpu.SMEM((4, 2) + TILE, jnp.int32), pltpu.SMEM((4, 2) + TILE, jnp.float32),
            I(2), V(2), pltpu.SMEM((2,) + TILE, jnp.int32), pltpu.SMEM((2,) + TILE, jnp.float32),
            D(2, 16), D(2, 16), D(2, 8), D(2, 16), D(2, 8), D(2, 4), D(2, 4), D(2, N_Z), D(2),
            D(2), D(2, N_Z), D(2, 2), D(2, 2), D(2, 2), D(2, 2), D(5),
        ],
        compiler_params=pltpu.CompilerParams(
            collective_id=0, has_side_effects=True, vmem_limit_bytes=60 * 2**20),
        name="two_sections",
    )(x, coupling, nsi, nsf, exports, ewi, ewf)
    return out[None]


def solution(mesh):
    placed = (
        P("panel", None, "lat", "lon"),
        P(),
        P("panel", "lat", "lon", None),
        P("panel", None, None, "lon", None),
        P("panel", None, None, "lon", None),
        P("panel", None, "lat", None, None),
        P("panel", None, "lat", None, None),
    )
    return jax.shard_map(
        local, mesh=mesh, in_specs=placed, out_specs=P("panel", None, "lat", "lon"), check_vma=False
    )
```

time: 117 us -> 97.2 us (0.83)
  the two profiles are of different devices: /device:TPU:28 before, /device:TPU:64 now
where the time goes in v1:
time: 97.2 us; the launch traced here: 97 us
  Pallas kernels  93.2 us (96%)
  local copies, waits for them, and re-layouts  3.76 us (4%)
    pallas_call x1, Pallas kernels, local(): pl.pallas_call(kernel, out_shape=jax.ShapeDtypeStruct(x.shape, jnp.float3...  93.2 us
    unnamed x1, local copies, waits for them, and re-layouts  3.76 us

profile of v1, /device:TPU:64, one launch (start us, length us, event | category | flops | bytes accessed | tf_op | source)
XLA Modules:
  0.0 97.0 jit_solution(13785898855955375616)
XLA Ops:
  0.0 93.2 %two_sections.1 = f32[8,64,1536]{2,1,0:T(8,128)} custom-call(f32[8,64,1536]{2,1,0:T(8,128)} %bitcast.16, f32[4,8,8]{2,1,0:T(8,128)} %coup_ref.1, s32[2,2,4,12]{3,2,1,0:T(4,128)} %bitcast.17, f32[2,2,2,12]{3,2,1,0:T(2,128)} %bitcast.19, s32[512]{0:T(512)} %bitcast.21, s32[2,2,4,64]{3,2,1,0:T(4,128)} %bitcast.18, f32[2,2,2,64]{3,2,1,0:T(2,128)} %bitcast.20), custom_call_target="tpu_custom_call" | custom-call | tf_op jit(solution)/shard_map/two_sections/pallas_call | solution.py:612
  93.2 3.8 %copy.9 = f32[1,8,64,1536]{3,2,1,0:T(8,128)} copy(f32[1,8,64,1536]{3,2,1,0:T(8,128)} %bitcast.15) | data formatting | bytes 6291456

commit v2 on v1

--- a/solution.py
+++ b/solution.py
@@ -27,14 +27,14 @@
     x_ref, coup_ref, nsi_ref, nsf_ref, exp_ref, ewi_ref, ewf_ref,
     out_ref,
     x_buf, q_init, q_mid, p_lat, p_lon, s_ref, res_ref, lhs_ref, isin_ref,
-    send_g, recv_g0, recv_g1, send_e, recv_e1, recv_e20, recv_e21, chunk, recv_n, summed,
+    send_g, g00, g01, g02, g03, g10, g11, g12, g13, send_e, recv_e1, recv_e20, recv_e21, chunk, recv_n, summed,
     lat_h, lon_h,
     own_i, own_w, got_i, got_w, adj_i, adj_w, smem_i, smem_w,
     adj_ei, adj_ew, smem_ei, smem_ew,
     g_send, g_recv, e1_send, e1_recv, i_send, i_recv, n_send, n_recv, f_send,
     e2_send, e2_recv, lat_send, lat_recv, lon_send, lon_recv, loc_sem,
 ):
-    recv_g = (recv_g0, recv_g1)
+    recv_g = ((g00, g01, g02, g03), (g10, g11, g12, g13))
     recv_e2 = (recv_e20, recv_e21)
     p = lax.axis_index("panel")
     y = lax.axis_index("lat")
@@ -164,7 +164,7 @@
             s = got_i[m]
             col = (s >> 2) & (N_LON - 1)
             k = (s >> 7) * 4 + (col & 3)
-            adj_i[m] = k * 16 + m * 4 + (s & 3)
+            adj_i[m] = k * 4 + (s & 3)
             adj_w[m] = jnp.where((col >> 2) == z, got_w[m], 0.0)
         copies = [pltpu.make_async_copy(adj_i, smem_i, loc_sem.at[3]),
                   pltpu.make_async_copy(adj_w, smem_w, loc_sem.at[4])]
@@ -262,22 +262,25 @@
         kpar = jnp.where(kup, 3 - ky, ky)
         return (jnp.where(kup, 96, 0) + kpar * 4 + (k % 4 + 2) % 4) * 4
 
-    def gather_g(st, cur, k):
-        first = group_of(k)
-        for m in range(4):
-            for s in range(4):
-                send_g[st, k, m * 4 + s] = column(cur, exp_ref[first + m * 32 + s])
-
-    def start_g(st, k):
+    def nth(n):
+        return lax.rem(z // 2 + 1 + n, 4)
+
+    def gather_g(st, cur, n, k):
+        first = group_of(k) + nth(n) * 32
+        for s in range(4):
+            send_g[st, n, k, s] = column(cur, exp_ref[first + s])
+
+    def start_g(st, n, k):
+        dst = recv_g[st][n].at[pl.ds(me_k * 4, 4)]
+
         @pl.when(k != me_k)
         def _():
-            rcopy(send_g.at[st, k], recv_g[st].at[me_k], g_send.at[st, k],
-                  g_recv.at[st, me_k], (p, k // 4, z * 4 + k % 4))
+            rcopy(send_g.at[st, n, k], dst, g_send.at[st, n, k],
+                  g_recv.at[st, n, me_k], (p, k // 4, z * 4 + k % 4))
 
         @pl.when(k == me_k)
         def _():
-            pltpu.make_async_copy(
-                send_g.at[st, k], recv_g[st].at[me_k], g_recv.at[st, me_k]).start()
+            pltpu.make_async_copy(send_g.at[st, n, k], dst, g_recv.at[st, n, me_k]).start()
 
     def gather_e(st, cur, t):
         first = ((t // 2) * N_LON + (t % 2) * (N_LON - 1)) * 4
@@ -324,8 +327,8 @@
             rcopy(cur.at[2:LAT_DEV + 2, 0:2], lon_h.at[st, 1], lon_send.at[st, 1],
                   lon_recv.at[st, 1], (p, y, b - 1))
 
-    def products(cur):
-        @pl.loop(0, LAT_DEV // 4)
+    def products(cur, quarter):
+        @pl.loop(quarter * (LAT_DEV // 16), (quarter + 1) * (LAT_DEV // 16))
         def _(c):
             i0 = c * 4
             cols = cur[pl.ds(i0 + 2, 4)].reshape((48,) + TILE)
@@ -370,32 +373,33 @@
             else:
                 res_ref[i] = 0.5 * q_init[i + 2] + 0.5 * (q0 + time_step * rate)
 
-    def aggregate(st):
+    def aggregate(st, n):
+        got = recv_g[st][n]
+
         @pl.loop(0, 16)
         def _(k):
-            wait_on(recv_g[st].at[k], g_recv.at[st, k])
-
-        @pl.loop(0, 4)
-        def _(m):
-            @pl.loop(0, LON_DEV)
-            def _(j):
-                for g in range(2):
-                    acc = jnp.zeros(TILE, jnp.float32)
-                    for t in range(4):
-                        idx = smem_i[m, g, t, j]
-                        acc = acc + smem_w[m, g, t, j] * recv_g[st][idx >> 4, idx & 15]
-                    chunk[st, m, g, j] = acc
-
-            zz = 2 * m + par
-
-            @pl.when(zz != z)
-            def _():
-                rcopy(chunk.at[st, m], recv_n.at[st, z], n_send.at[st, m], n_recv.at[st, z],
-                      (p, y, zz * 4 + w))
-
-            @pl.when(zz == z)
-            def _():
-                pltpu.make_async_copy(chunk.at[st, m], recv_n.at[st, z], n_recv.at[st, z]).start()
+            wait_on(got.at[pl.ds(k * 4, 4)], g_recv.at[st, n, k])
+
+        m = nth(n)
+
+        @pl.loop(0, LON_DEV)
+        def _(j):
+            for g in range(2):
+                acc = jnp.zeros(TILE, jnp.float32)
+                for t in range(4):
+                    acc = acc + smem_w[m, g, t, j] * got[smem_i[m, g, t, j]]
+                chunk[st, n, g, j] = acc
+
+        zz = 2 * m + par
+
+        @pl.when(zz != z)
+        def _():
+            rcopy(chunk.at[st, n], recv_n.at[st, z], n_send.at[st, n], n_recv.at[st, z],
+                  (p, y, zz * 4 + w))
+
+        @pl.when(zz == z)
+        def _():
+            pltpu.make_async_copy(chunk.at[st, n], recv_n.at[st, z], n_recv.at[st, z]).start()
 
     def sum_over_z(st):
         @pl.when(is_sum)
@@ -495,9 +499,10 @@
     def _(t):
         gather_e(0, q_init, t)
 
-    @pl.loop(0, 16)
-    def _(n):
-        gather_g(0, q_init, n)
+    for n in range(4):
+        @pl.loop(0, 16)
+        def _(k):
+            gather_g(0, q_init, n, k)
 
     prepare_indices()
     build_lhs()
@@ -514,18 +519,25 @@
         if st == 0:
             send_indices()
 
-        @pl.loop(0, 16)
-        def _(n):
-            k = turn(n)
-            if st == 1:
-                gather_g(st, cur, k)
-            start_g(st, k)
+        for n in range(4):
+            @pl.loop(0, 16)
+            def _(r):
+                k = turn(r)
+                if st == 1:
+                    gather_g(st, cur, n, k)
+                start_g(st, n, k)
 
         if st == 0:
             adjust_indices()
+        products(cur, 0)
         forward_ew(st)
-        products(cur)
-        aggregate(st)
+        products(cur, 1)
+        aggregate(st, 0)
+        products(cur, 2)
+        aggregate(st, 1)
+        products(cur, 3)
+        aggregate(st, 2)
+        aggregate(st, 3)
         halos(st, cur)
         stencil(st, cur)
         sum_over_z(st)
@@ -550,11 +562,12 @@
             wait_on(own_w, i_send.at[1, zz])
 
     for st in range(2):
-        @pl.loop(0, 16)
-        def _(k):
-            @pl.when(k != me_k)
-            def _():
-                wait_on(send_g.at[st, k], g_send.at[st, k])
+        for n in range(4):
+            @pl.loop(0, 16)
+            def _(k):
+                @pl.when(k != me_k)
+                def _():
+                    wait_on(send_g.at[st, n, k], g_send.at[st, n, k])
 
         @pl.loop(0, 8)
         def _(t):
@@ -562,11 +575,10 @@
             def _():
                 wait_on(send_e.at[st, t], e1_send.at[st, t])
 
-        @pl.loop(0, 4)
-        def _(m):
-            @pl.when(2 * m + par != z)
+        for n in range(4):
+            @pl.when(2 * nth(n) + par != z)
             def _():
-                wait_on(chunk.at[st, m], n_send.at[st, m])
+                wait_on(chunk.at[st, n], n_send.at[st, n])
 
         @pl.when(is_sum)
         def _():
@@ -619,13 +631,13 @@
             V(LAT_DEV + 4, LON_DEV), V(LAT_DEV + 4, LON_DEV), V(LAT_DEV + 4, LON_DEV),
             V(LAT_DEV, LON_DEV), V(LAT_DEV, LON_DEV), V(LAT_DEV, LON_DEV),
             pltpu.VMEM((448, 192), jnp.bfloat16), pltpu.VMEM((LAT_DEV, NR), jnp.float32),
-            V(2, 16, 16), V(16, 16), V(16, 16), V(2, 8, 4), V(2, 16, 4), V(N_Z, 16, 4), V(N_Z, 16, 4),
+            V(2, 4, 16, 4)] + [V(64)] * 8 + [V(2, 8, 4), V(2, 16, 4), V(N_Z, 16, 4), V(N_Z, 16, 4),
             V(2, 4, 2, LON_DEV), V(2, N_Z, 2, LON_DEV), V(2, 2, LON_DEV),
             V(2, 2, 2, LON_DEV), V(2, 2, LAT_DEV, 2),
             I(2), V(2), I(4, 2), V(4, 2), I(4, 2), V(4, 2),
             pltpu.SMEM((4, 2) + TILE, jnp.int32), pltpu.SMEM((4, 2) + TILE, jnp.float32),
             I(2), V(2), pltpu.SMEM((2,) + TILE, jnp.int32), pltpu.SMEM((2,) + TILE, jnp.float32),
-            D(2, 16), D(2, 16), D(2, 8), D(2, 16), D(2, 8), D(2, 4), D(2, 4), D(2, N_Z), D(2),
+            D(2, 4, 16), D(2, 4, 16), D(2, 8), D(2, 16), D(2, 8), D(2, 4), D(2, 4), D(2, N_Z), D(2),
             D(2), D(2, N_Z), D(2, 2), D(2, 2), D(2, 2), D(2, 2), D(5),
         ],
         compiler_params=pltpu.CompilerParams(

time: 97.2 us -> 95 us (0.977)
  Pallas kernels: 93.2 us -> 91 us
    pallas_call x1, Pallas kernels: 93.2 us -> 91 us  [local(): pl.pallas_call(kernel, out_shape=jax.ShapeDtypeStruct(x.shape, jnp.float3...]
where the time goes in v2:
time: 95 us; the launch traced here: 94.8 us
  Pallas kernels  91 us (96%)
  local copies, waits for them, and re-layouts  3.76 us (4%)
    pallas_call x1, Pallas kernels, local(): pl.pallas_call(kernel, out_shape=jax.ShapeDtypeStruct(x.shape, jnp.float3...  91 us
    unnamed x1, local copies, waits for them, and re-layouts  3.76 us

profile of v2, /device:TPU:64, one launch (start us, length us, event | category | flops | bytes accessed | tf_op | source)
XLA Modules:
  0.0 94.8 jit_solution(725365035583114964)
XLA Ops:
  0.0 91.0 %two_sections.1 = f32[8,64,1536]{2,1,0:T(8,128)} custom-call(f32[8,64,1536]{2,1,0:T(8,128)} %bitcast.16, f32[4,8,8]{2,1,0:T(8,128)} %coup_ref.1, s32[2,2,4,12]{3,2,1,0:T(4,128)} %bitcast.17, f32[2,2,2,12]{3,2,1,0:T(2,128)} %bitcast.19, s32[512]{0:T(512)} %bitcast.21, s32[2,2,4,64]{3,2,1,0:T(4,128)} %bitcast.18, f32[2,2,2,64]{3,2,1,0:T(2,128)} %bitcast.20), custom_call_target="tpu_custom_call" | custom-call | tf_op jit(solution)/shard_map/two_sections/pallas_call | solution.py:624
  91.0 3.8 %copy.9 = f32[1,8,64,1536]{3,2,1,0:T(8,128)} copy(f32[1,8,64,1536]{3,2,1,0:T(8,128)} %bitcast.15) | data formatting | bytes 6291456

commit v3 on v2

--- a/solution.py
+++ b/solution.py
@@ -26,7 +26,7 @@
 def kernel(
     x_ref, coup_ref, nsi_ref, nsf_ref, exp_ref, ewi_ref, ewf_ref,
     out_ref,
-    x_buf, q_init, q_mid, p_lat, p_lon, s_ref, res_ref, lhs_ref, isin_ref,
+    q_init, q_mid, p_lat, p_lon, s_ref, res_ref, lhs_ref, isin_ref,
     send_g, g00, g01, g02, g03, g10, g11, g12, g13, send_e, recv_e1, recv_e20, recv_e21, chunk, recv_n, summed,
     lat_h, lon_h,
     own_i, own_w, got_i, got_w, adj_i, adj_w, smem_i, smem_w,
@@ -56,7 +56,7 @@
     ew_side = jnp.where(b == 0, 0, 1)
     star = jnp.where(y == 0, z % 2, 3 - z % 2)
 
-    x_copy = pltpu.make_async_copy(x_ref, x_buf, loc_sem.at[0])
+    x_copy = pltpu.make_async_copy(x_ref, out_ref, loc_sem.at[0])
     x_copy.start()
 
     bar = pltpu.get_barrier_semaphore()
@@ -184,7 +184,7 @@
         def _(ib):
             i0 = pl.multiple_of(ib * 8, 8)
             for j in range(LON_DEV):
-                v = x_buf[:, pl.ds(i0, 8), j * NR:(j + 1) * NR]
+                v = out_ref[:, pl.ds(i0, 8), j * NR:(j + 1) * NR]
                 q_init[pl.ds(i0 + 2, 8), j] = jnp.swapaxes(v, 0, 1)
 
     radius = inner_radius + (1.0 - inner_radius) * (
@@ -617,7 +617,7 @@
 
     vm = pl.BlockSpec(memory_space=pltpu.VMEM)
     sm = pl.BlockSpec(memory_space=pltpu.SMEM)
-    hbm = pl.BlockSpec(memory_space=pl.ANY)
+    hbm = pl.BlockSpec(memory_space=pltpu.HBM)
     V = lambda *shape: pltpu.VMEM(shape + TILE, jnp.float32)
     I = lambda *shape: pltpu.VMEM(shape + TILE, jnp.int32)
     D = lambda *shape: pltpu.SemaphoreType.DMA(shape)
@@ -627,7 +627,6 @@
         in_specs=[hbm, vm, vm, vm, sm, vm, vm],
         out_specs=vm,
         scratch_shapes=[
-            pltpu.VMEM(x.shape, jnp.float32),
             V(LAT_DEV + 4, LON_DEV), V(LAT_DEV + 4, LON_DEV), V(LAT_DEV + 4, LON_DEV),
             V(LAT_DEV, LON_DEV), V(LAT_DEV, LON_DEV), V(LAT_DEV, LON_DEV),
             pltpu.VMEM((448, 192), jnp.bfloat16), pltpu.VMEM((LAT_DEV, NR), jnp.float32),
@@ -641,7 +640,7 @@
             D(2), D(2, N_Z), D(2, 2), D(2, 2), D(2, 2), D(2, 2), D(5),
         ],
         compiler_params=pltpu.CompilerParams(
-            collective_id=0, has_side_effects=True, vmem_limit_bytes=60 * 2**20),
+            collective_id=0, has_side_effects=True, vmem_limit_bytes=49 * 2**20),
         name="two_sections",
     )(x, coupling, nsi, nsf, exports, ewi, ewf)
     return out[None]

time: 95 us -> 95.3 us (level)
  local copies, waits for them, and re-layouts: 3.76 us -> 5.83 us
  Pallas kernels: 91 us -> 89.1 us
    unnamed x1 -> x13, local copies, waits for them, and re-layouts: 3.76 us -> 5.83 us
    pallas_call x1, Pallas kernels: 91 us -> 89.1 us  [local(): pl.pallas_call(kernel, out_shape=jax.ShapeDtypeStruct(x.shape, jnp.float3...]
where the time goes in v3:
time: 95.3 us; the launch traced here: 95 us
  Pallas kernels  89.1 us (93%)
  local copies, waits for them, and re-layouts  5.83 us (6%)
    pallas_call x1, Pallas kernels, local(): pl.pallas_call(kernel, out_shape=jax.ShapeDtypeStruct(x.shape, jnp.float3...  89.1 us
    unnamed x13, local copies, waits for them, and re-layouts  5.83 us

profile of v3, /device:TPU:64, one launch (start us, length us, event | category | flops | bytes accessed | tf_op | source)
XLA Modules:
  0.0 95.0 jit_solution(11194549953494692931)
XLA Ops:
  0.0 0.0 copy-start
  0.0 0.7 copy-done
  0.7 0.0 copy-start.1
  0.7 0.7 copy-done.1
  1.4 0.0 copy-start.2
  1.4 0.7 copy-done.2
  2.1 0.0 copy-start.3
  2.1 0.7 copy-done.3
  2.8 0.0 copy-start.4
  2.8 0.7 copy-done.4
  3.5 0.0 copy-start.5
  3.5 0.7 copy-done.5
  4.2 89.1 %two_sections.1 = f32[8,64,1536]{2,1,0:T(8,128)S(1)} custom-call(f32[8,64,1536]{2,1,0:T(8,128)} %bitcast.21, f32[4,8,8]{2,1,0:T(8,128)S(1)} %copy-done, s32[2,2,4,12]{3,2,1,0:T(4,128)S(1)} %bitcast.16, f32[2,2,2,12]{3,2,1,0:T(2,128)S(1)} %bitcast.18, s32[512]{0:T(512)S(1)} %bitcast.20, s32[2,2,4,64]{3,2,1,0:T(4,128)S(1)} %bitcast.17, ...), custom_call_target="tpu_custom_call" | custom-call | tf_op jit(solution)/shard_map/two_sections/pallas_call | solution.py:624
  93.3 1.7 %copy.9 = f32[1,8,64,1536]{3,2,1,0:T(8,128)} copy(f32[1,8,64,1536]{3,2,1,0:T(8,128)S(1)} %bitcast.15) | data formatting | bytes 6291456
Async XLA Ops:
  0.0 0.7 copy-start
  0.7 0.7 copy-start.1
  1.4 0.7 copy-start.2
  2.1 0.7 copy-start.3
  2.8 0.7 copy-start.4
  3.5 0.7 copy-start.5

commit v4 on v2

--- a/solution.py
+++ b/solution.py
@@ -527,10 +527,10 @@
                     gather_g(st, cur, n, k)
                 start_g(st, n, k)
 
+        forward_ew(st)
         if st == 0:
             adjust_indices()
         products(cur, 0)
-        forward_ew(st)
         products(cur, 1)
         aggregate(st, 0)
         products(cur, 2)

time: 95 us -> 95.2 us (level)
  no operation moved by 1% of the time
where the time goes in v4:
time: 95.2 us; the launch traced here: 95 us
  Pallas kernels  91.2 us (96%)
  local copies, waits for them, and re-layouts  3.76 us (4%)
    pallas_call x1, Pallas kernels, local(): pl.pallas_call(kernel, out_shape=jax.ShapeDtypeStruct(x.shape, jnp.float3...  91.2 us
    unnamed x1, local copies, waits for them, and re-layouts  3.76 us

profile of v4, /device:TPU:64, one launch (start us, length us, event | category | flops | bytes accessed | tf_op | source)
XLA Modules:
  0.0 95.0 jit_solution(14442641905927298778)
XLA Ops:
  0.0 91.2 %two_sections.1 = f32[8,64,1536]{2,1,0:T(8,128)} custom-call(f32[8,64,1536]{2,1,0:T(8,128)} %bitcast.16, f32[4,8,8]{2,1,0:T(8,128)} %coup_ref.1, s32[2,2,4,12]{3,2,1,0:T(4,128)} %bitcast.17, f32[2,2,2,12]{3,2,1,0:T(2,128)} %bitcast.19, s32[512]{0:T(512)} %bitcast.21, s32[2,2,4,64]{3,2,1,0:T(4,128)} %bitcast.18, f32[2,2,2,64]{3,2,1,0:T(2,128)} %bitcast.20), custom_call_target="tpu_custom_call" | custom-call | tf_op jit(solution)/shard_map/two_sections/pallas_call | solution.py:624
  91.2 3.8 %copy.9 = f32[1,8,64,1536]{3,2,1,0:T(8,128)} copy(f32[1,8,64,1536]{3,2,1,0:T(8,128)} %bitcast.15) | data formatting | bytes 6291456

commit v5 on v2

--- a/solution.py
+++ b/solution.py
@@ -382,7 +382,7 @@
 
         m = nth(n)
 
-        @pl.loop(0, LON_DEV)
+        @pl.loop(0, LON_DEV, unroll=4)
         def _(j):
             for g in range(2):
                 acc = jnp.zeros(TILE, jnp.float32)
@@ -433,7 +433,7 @@
             def _(zz):
                 wait_on(recv_e2[st].at[zz], e2_recv.at[st, zz])
 
-            @pl.loop(0, LAT_DEV)
+            @pl.loop(0, LAT_DEV, unroll=4)
             def _(i):
                 for g in range(2):
                     acc = jnp.zeros(TILE, jnp.float32)
@@ -475,19 +475,19 @@
     def correct_lon(st):
         dst, off, sc, sc2 = target(st)
 
-        @pl.loop(0, LAT_DEV // 4)
+        @pl.loop(0, LAT_DEV // 16)
         def _(c):
-            i0 = c * 4
-            west = lon_h[st, 0, pl.ds(i0, 4)].reshape((8,) + TILE)
-            east = lon_h[st, 1, pl.ds(i0, 4)].reshape((8,) + TILE)
-            both = unsplit(mixed(slice(384, 448), jnp.concatenate([west, east], axis=0)), 2)
-            for n in range(4):
+            i0 = c * 16
+            west = lon_h[st, 0, pl.ds(i0, 16)].reshape((32,) + TILE)
+            east = lon_h[st, 1, pl.ds(i0, 16)].reshape((32,) + TILE)
+            both = unsplit(mixed(slice(384, 448), jnp.concatenate([west, east], axis=0)), 8)
+            for n in range(16):
                 i = i0 + n
                 si = inv_sin(i)
                 a1 = sc * si
                 a2 = sc2 * (si * si)
                 w2, w1, pw2, pw1 = west[2 * n], west[2 * n + 1], both[2 * n], both[2 * n + 1]
-                e1, e2, pe1, pe2 = east[2 * n], east[2 * n + 1], both[8 + 2 * n], both[9 + 2 * n]
+                e1, e2, pe1, pe2 = east[2 * n], east[2 * n + 1], both[32 + 2 * n], both[33 + 2 * n]
                 dst[off + i, 0] += a1 * (pw2 - 8.0 * pw1) + a2 * (16.0 * w1 - w2)
                 dst[off + i, 1] += a1 * pw1 - a2 * w1
                 dst[off + i, 11] += a1 * (8.0 * pe1 - pe2) + a2 * (16.0 * e1 - e2)

time: 95 us -> 99.1 us (1.043)
  the two profiles are of different devices: /device:TPU:64 before, /device:TPU:199 now
where the time goes in v5:
time: 99.1 us; the launch traced here: 98.9 us
  Pallas kernels  95.2 us (96%)
  local copies, waits for them, and re-layouts  3.76 us (4%)
    pallas_call x1, Pallas kernels, local(): pl.pallas_call(kernel, out_shape=jax.ShapeDtypeStruct(x.shape, jnp.float3...  95.2 us
    unnamed x1, local copies, waits for them, and re-layouts  3.76 us

profile of v5, /device:TPU:199, one launch (start us, length us, event | category | flops | bytes accessed | tf_op | source)
XLA Modules:
  0.0 98.9 jit_solution(11948835490650846829)
XLA Ops:
  0.0 95.2 %two_sections.1 = f32[8,64,1536]{2,1,0:T(8,128)} custom-call(f32[8,64,1536]{2,1,0:T(8,128)} %bitcast.16, f32[4,8,8]{2,1,0:T(8,128)} %coup_ref.1, s32[2,2,4,12]{3,2,1,0:T(4,128)} %bitcast.17, f32[2,2,2,12]{3,2,1,0:T(2,128)} %bitcast.19, s32[512]{0:T(512)} %bitcast.21, s32[2,2,4,64]{3,2,1,0:T(4,128)} %bitcast.18, f32[2,2,2,64]{3,2,1,0:T(2,128)} %bitcast.20), custom_call_target="tpu_custom_call" | custom-call | tf_op jit(solution)/shard_map/two_sections/pallas_call | solution.py:624
  95.2 3.8 %copy.9 = f32[1,8,64,1536]{3,2,1,0:T(8,128)} copy(f32[1,8,64,1536]{3,2,1,0:T(8,128)} %bitcast.15) | data formatting | bytes 6291456

commit v6 on v2

--- a/solution.py
+++ b/solution.py
@@ -26,7 +26,7 @@
 def kernel(
     x_ref, coup_ref, nsi_ref, nsf_ref, exp_ref, ewi_ref, ewf_ref,
     out_ref,
-    x_buf, q_init, q_mid, p_lat, p_lon, s_ref, res_ref, lhs_ref, isin_ref,
+    x_buf, q_init, q_mid, p_lat, p_lon, s_ref, lhs_ref, isin_ref,
     send_g, g00, g01, g02, g03, g10, g11, g12, g13, send_e, recv_e1, recv_e20, recv_e21, chunk, recv_n, summed,
     lat_h, lon_h,
     own_i, own_w, got_i, got_w, adj_i, adj_w, smem_i, smem_w,
@@ -371,7 +371,7 @@
             if st == 0:
                 q_mid[i + 2] = q0 + time_step * rate
             else:
-                res_ref[i] = 0.5 * q_init[i + 2] + 0.5 * (q0 + time_step * rate)
+                out_ref[i] = 0.5 * q_init[i + 2] + 0.5 * (q0 + time_step * rate)
 
     def aggregate(st, n):
         got = recv_g[st][n]
@@ -458,7 +458,7 @@
     def target(st):
         if st == 0:
             return q_mid, 2, time_step * ct, time_step * ct2
-        return res_ref, 0, 0.5 * time_step * ct, 0.5 * time_step * ct2
+        return out_ref, 0, 0.5 * time_step * ct, 0.5 * time_step * ct2
 
     def correct_lat(st):
         dst, off, sc, sc2 = target(st)
@@ -547,13 +547,6 @@
         wait_lat(st)
         correct_lat(st)
 
-    @pl.loop(0, LAT_DEV // 8)
-    def _(ib):
-        i0 = pl.multiple_of(ib * 8, 8)
-        for j in range(LON_DEV):
-            v = res_ref[pl.ds(i0, 8), j]
-            out_ref[:, pl.ds(i0, 8), j * NR:(j + 1) * NR] = jnp.swapaxes(v, 0, 1)
-
     @pl.when(is_sum)
     def _():
         @pl.loop(0, N_Z)
@@ -603,6 +596,13 @@
         @pl.when(y > 0)
         def _():
             wait_on(lat_h.at[st, 1], lat_send.at[st, 1])
+
+
+def fields_first(cells_ref, out_ref):
+    for ib in range(cells_ref.shape[0] // 8):
+        part = slice(8 * ib, 8 * ib + 8)
+        for j in range(LON_DEV):
+            out_ref[:, part, j * NR:(j + 1) * NR] = jnp.swapaxes(cells_ref[part, j], 0, 1)
 
 
 def local(
@@ -623,13 +623,13 @@
     D = lambda *shape: pltpu.SemaphoreType.DMA(shape)
     out = pl.pallas_call(
         kernel,
-        out_shape=jax.ShapeDtypeStruct(x.shape, jnp.float32),
+        out_shape=jax.ShapeDtypeStruct((LAT_DEV, LON_DEV) + TILE, jnp.float32),
         in_specs=[hbm, vm, vm, vm, sm, vm, vm],
         out_specs=vm,
         scratch_shapes=[
             pltpu.VMEM(x.shape, jnp.float32),
             V(LAT_DEV + 4, LON_DEV), V(LAT_DEV + 4, LON_DEV), V(LAT_DEV + 4, LON_DEV),
-            V(LAT_DEV, LON_DEV), V(LAT_DEV, LON_DEV), V(LAT_DEV, LON_DEV),
+            V(LAT_DEV, LON_DEV), V(LAT_DEV, LON_DEV),
             pltpu.VMEM((448, 192), jnp.bfloat16), pltpu.VMEM((LAT_DEV, NR), jnp.float32),
             V(2, 4, 16, 4)] + [V(64)] * 8 + [V(2, 8, 4), V(2, 16, 4), V(N_Z, 16, 4), V(N_Z, 16, 4),
             V(2, 4, 2, LON_DEV), V(2, N_Z, 2, LON_DEV), V(2, 2, LON_DEV),
@@ -644,7 +644,15 @@
             collective_id=0, has_side_effects=True, vmem_limit_bytes=60 * 2**20),
         name="two_sections",
     )(x, coupling, nsi, nsf, exports, ewi, ewf)
-    return out[None]
+    rows = 16
+    return pl.pallas_call(
+        fields_first,
+        grid=(LAT_DEV // rows,),
+        out_shape=jax.ShapeDtypeStruct(x.shape, jnp.float32),
+        in_specs=[pl.BlockSpec((rows, LON_DEV) + TILE, lambda i: (i, 0, 0, 0))],
+        out_specs=pl.BlockSpec((FIELDS, rows, LON_DEV * NR), lambda i: (0, i, 0)),
+        name="fields_first",
+    )(out)[None]
 
 
 def solution(mesh):

time: 95 us -> 95 us (level)
  Pallas kernels: 91 us -> 94.8 us
  local copies, waits for them, and re-layouts: 3.76 us -> 0 us
    pallas_call x1 -> x2, Pallas kernels: 91 us -> 94.8 us  [the longest x1 90.4 us: local(): pl.pallas_call(kernel, out_shape=jax.ShapeDtypeStruct((LAT_DEV, LON_DEV)...]
    unnamed x1 -> x0, local copies, waits for them, and re-layouts: 3.76 us -> none
where the time goes in v6:
time: 95 us; the launch traced here: 94.8 us
  Pallas kernels  94.8 us (100%)
    pallas_call x1, Pallas kernels, local(): pl.pallas_call(kernel, out_shape=jax.ShapeDtypeStruct((LAT_DEV, LON_DEV)...  90.4 us
    pallas_call x1, Pallas kernels, local(): pl.pallas_call(fields_first, grid=(LAT_DEV // rows,), out_shape=jax.Shape...  4.38 us

profile of v6, /device:TPU:64, one launch (start us, length us, event | category | flops | bytes accessed | tf_op | source)
XLA Modules:
  0.0 94.8 jit_solution(3708694107052709719)
XLA Ops:
  0.0 90.4 %two_sections.1.cells_ref = f32[64,12,8,128]{3,2,1,0:T(8,128)} custom-call(f32[8,64,1536]{2,1,0:T(8,128)} %bitcast.15, f32[4,8,8]{2,1,0:T(8,128)} %coup_ref.1, s32[2,2,4,12]{3,2,1,0:T(4,128)} %bitcast.16, f32[2,2,2,12]{3,2,1,0:T(2,128)} %bitcast.18, s32[512]{0:T(512)} %bitcast.20, s32[2,2,4,64]{3,2,1,0:T(4,128)} %bitcast.17, f32[2,2,2,64]{3,2,1,0:T(2,128)} %bitcast.19), custom_call_target="tpu_custom_call" | custom-call | tf_op jit(solution)/shard_map/two_sections/pallas_call | solution.py:624
  90.4 4.4 %fields_first.1 = f32[8,64,1536]{2,1,0:T(8,128)} custom-call(f32[64,12,8,128]{3,2,1,0:T(8,128)} %two_sections.1.cells_ref), custom_call_target="tpu_custom_call" | custom-call | tf_op jit(solution)/shard_map/fields_first/pallas_call | solution.py:648
